TPU v7x, 32 devices: a whole 2x2x4 slice. The times are simulated.
32 devices in a mesh: dp: 2 (over x), fsdp: 16 (over z, y, core).
Axes of the slice: x: 2, y: 2, z: 4, core: 2. Of those that a mesh axis runs over, the one named last changes fastest.
Arguments:
- hidden: bfloat16 [64, 64, 768], P(('dp', 'fsdp')), may hold values from -6 to 6
- lengths: int32 [64], P(('dp', 'fsdp')), may hold values from 5 to 32, as said below
- features: bfloat16 [64, 257, 1408], P(('dp', 'fsdp')), may hold values from -6 to 6
- cotangent: bfloat16 [64, 64, 768], P(('dp', 'fsdp')), may hold values from -6 to 6
- self_params: bfloat16 [2363392], P('fsdp')
- cross_params: bfloat16 [3346432], P('fsdp')
- ffn_params: bfloat16 [9449472], P('fsdp')
Outputs:
- mixed: bfloat16 [64, 64, 768], P(('dp', 'fsdp'))
- hidden_grad: bfloat16 [64, 64, 768], P(('dp', 'fsdp'))
- self_grad: float32 [2363392], P('fsdp')
- cross_grad: float32 [3346432], P('fsdp')
- ffn_grad: float32 [9449472], P('fsdp')
Inputs may be any that keep to these rules, and one draw needn't show every extreme that they name: lengths lie between 5 and 32; some item of every draw has 32.
All inputs are finite; a program needn't handle non-finite values.
Results may differ from a plain program's by a relative error of at most 0.017.
Values may be sent and summed in bfloat16 or wider, within the bound.
A program may use at most 384 MiB of HBM per device.

v0:
```python
from functools import partial
import math
import jax
import jax.numpy as jnp
from jax import lax
from jax.sharding import PartitionSpec as P

D = 768
HEADS = 12
HDIM = 64
F = 3072
E = 1408
NQ = 32
EPS = 1e-06
SCALE = 0.125


def self_layout():
    return [(D, D)] * 4 + [(D,)] * 5


def cross_layout():
    return [(D, D), (E, D), (E, D), (D, D)] + [(D,)] * 5


def ffn_layout():
    return [(D, F), (F,), (F, D), (D,), (D,), (D,)] * 2


def split_flat(flat_vec, layouts):
    pieces = []
    offset = 0
    for layout in layouts:
        amount = math.prod(layout)
        pieces.append(flat_vec[offset : offset + amount].reshape(layout))
        offset = offset + amount
    return pieces


def join_flat(pieces, length):
    flat_vec = jnp.concatenate([piece.reshape(-1) for piece in pieces])
    return jnp.pad(flat_vec, (0, length - flat_vec.shape[0]))


def regroup(flat_vec):
    groups = lax.axis_size("fsdp")
    replicas = lax.axis_size("dp")
    return flat_vec.reshape(groups, replicas, -1).transpose(1, 0, 2).reshape(-1)


def matmul(left, right):
    return jnp.dot(left, right, preferred_element_type=jnp.float32)


def matmul_left(left, right):
    return lax.dot_general(
        left, right, (((0,), (0,)), ((), ())), preferred_element_type=jnp.float32
    )


def matmul_right(left, right):
    return lax.dot_general(
        left, right, (((1,), (1,)), ((), ())), preferred_element_type=jnp.float32
    )


def column_sum(values):
    return jnp.sum(values.astype(jnp.float32), 0)


def layer_norm(values, gain, shift):
    average = jnp.mean(values, -1, keepdims=True)
    centered = values - average
    variance = jnp.mean(centered * centered, -1, keepdims=True)
    return centered * lax.rsqrt(variance + EPS) * gain + shift


def norm_backward(summed, gain, shift, grad_out):
    _, norm_pull = jax.vjp(layer_norm, summed, gain.astype(jnp.float32), shift.astype(jnp.float32))
    return norm_pull(grad_out)


def heads(rows, items):
    return rows.reshape(items, -1, HEADS, HDIM)


def score_block(query, keys, mask):
    scores = jnp.einsum("iqhd,ikhd->ihqk", query, keys, preferred_element_type=jnp.float32) * SCALE
    if mask is not None:
        scores = jnp.where(mask, scores, -1e30)
    return scores


def attend(query, keys, values, mask):
    scores = score_block(query, keys, mask)
    top_sum = jax.nn.logsumexp(scores, axis=-1)
    probs = jnp.exp(scores - top_sum[..., None]).astype(jnp.bfloat16)
    context = jnp.einsum("ihqk,ikhd->iqhd", probs, values, preferred_element_type=jnp.float32)
    return (context, top_sum)


def attend_back(query, keys, values, mask, top_sum, grad_context):
    probs = jnp.exp(score_block(query, keys, mask) - top_sum[..., None])
    grad_probs = jnp.einsum(
        "iqhd,ikhd->ihqk", grad_context, values, preferred_element_type=jnp.float32
    )
    inner = jnp.sum(probs * grad_probs, -1, keepdims=True)
    grad_scores = (probs * (grad_probs - inner)).astype(jnp.bfloat16)
    grad_query = (
        jnp.einsum("ihqk,ikhd->iqhd", grad_scores, keys, preferred_element_type=jnp.float32) * SCALE
    )
    grad_keys = (
        jnp.einsum("ihqk,iqhd->ikhd", grad_scores, query, preferred_element_type=jnp.float32)
        * SCALE
    )
    grad_values = jnp.einsum(
        "ihqk,iqhd->ikhd",
        probs.astype(jnp.bfloat16),
        grad_context,
        preferred_element_type=jnp.float32,
    )
    return (grad_query, grad_keys, grad_values)


def linear_back(inputs, weight, grad_out):
    return (matmul_left(inputs, grad_out), column_sum(grad_out), matmul_right(grad_out, weight))


def ffn_forward(rows, params):
    w_in, b_in, w_out, b_out, gain, shift = params
    rows_low = rows.astype(jnp.bfloat16)
    hidden_pre = matmul(rows_low, w_in) + b_in
    activated = jax.nn.gelu(hidden_pre, approximate=True).astype(jnp.bfloat16)
    summed = rows + (matmul(activated, w_out) + b_out)
    final = layer_norm(summed, gain.astype(jnp.float32), shift.astype(jnp.float32))
    return (final, (rows_low, hidden_pre, activated, summed))


def ffn_backward(grad_out, kept, params):
    w_in, b_in, w_out, b_out, gain, shift = params
    rows_low, hidden_pre, activated, summed = kept
    grad_sum, grad_gain, grad_shift = norm_backward(summed, gain, shift, grad_out)
    grad_branch = grad_sum.astype(jnp.bfloat16)
    grad_w_out, grad_b_out, grad_act = linear_back(activated, w_out, grad_branch)
    _, gelu_pull = jax.vjp(partial(jax.nn.gelu, approximate=True), hidden_pre)
    grad_pre = gelu_pull(grad_act)[0].astype(jnp.bfloat16)
    grad_w_in, grad_b_in, grad_rows = linear_back(rows_low, w_in, grad_pre)
    return (
        grad_sum + grad_rows,
        [grad_w_in, grad_b_in, grad_w_out, grad_b_out, grad_gain, grad_shift],
    )


def per_device(hidden, lengths, features, cotangent, self_params, cross_params, ffn_params):
    items, seq, width = hidden.shape
    self_full = lax.all_gather(self_params, "fsdp", axis=0, tiled=True)
    self_parts = split_flat(self_full, self_layout())
    w_q, w_k, w_v, w_o, b_q, b_v, b_o, gain_one, shift_one = self_parts
    positions = jnp.arange(seq)
    rows_at = positions[:, None]
    cols_at = positions[None, :]
    allowed = (cols_at < NQ)[None] | ((rows_at >= NQ) & (cols_at <= rows_at))[None] & (
        cols_at[None] < NQ + lengths[:, None, None]
    )
    allowed = allowed[:, None]
    inputs = hidden.reshape(-1, width)
    query_low = (matmul(inputs, w_q) + b_q).astype(jnp.bfloat16)
    key_low = matmul(inputs, w_k).astype(jnp.bfloat16)
    value_low = (matmul(inputs, w_v) + b_v).astype(jnp.bfloat16)
    context, self_top = attend(
        heads(query_low, items), heads(key_low, items), heads(value_low, items), allowed
    )
    context_low = context.reshape(-1, width).astype(jnp.bfloat16)
    summed_one = inputs.astype(jnp.float32) + (matmul(context_low, w_o) + b_o)
    first = layer_norm(summed_one, gain_one.astype(jnp.float32), shift_one.astype(jnp.float32))
    first_items = first.reshape(items, seq, width)
    query_rows = first_items[:, :NQ].reshape(-1, width)
    text_rows = first_items[:, NQ:].reshape(-1, width)
    cross_full = lax.all_gather(cross_params, "fsdp", axis=0, tiled=True)
    cross_parts = split_flat(cross_full, cross_layout())
    cross_wq, cross_wk, cross_wv, cross_wo, cross_bq, cross_bv, cross_bo, gain_two, shift_two = (
        cross_parts
    )
    query_in = query_rows.astype(jnp.bfloat16)
    image_rows = features.reshape(-1, features.shape[-1])
    cross_query = (matmul(query_in, cross_wq) + cross_bq).astype(jnp.bfloat16)
    cross_key = matmul(image_rows, cross_wk).astype(jnp.bfloat16)
    cross_value = (matmul(image_rows, cross_wv) + cross_bv).astype(jnp.bfloat16)
    cross_context, cross_top = attend(
        heads(cross_query, items), heads(cross_key, items), heads(cross_value, items), None
    )
    cross_low = cross_context.reshape(-1, width).astype(jnp.bfloat16)
    summed_two = query_rows + (matmul(cross_low, cross_wo) + cross_bo)
    second = layer_norm(summed_two, gain_two.astype(jnp.float32), shift_two.astype(jnp.float32))
    ffn_full = lax.all_gather(ffn_params, "fsdp", axis=0, tiled=True)
    ffn_parts = split_flat(ffn_full, ffn_layout())
    query_final, query_kept = ffn_forward(second, ffn_parts[:6])
    text_final, text_kept = ffn_forward(text_rows, ffn_parts[6:])
    mixed = jnp.concatenate(
        [query_final.reshape(items, NQ, width), text_final.reshape(items, -1, width)], 1
    ).astype(jnp.bfloat16)
    grad_items = cotangent.astype(jnp.float32)
    grad_query_final = grad_items[:, :NQ].reshape(-1, width)
    grad_text_final = grad_items[:, NQ:].reshape(-1, width)
    ffn_back = split_flat(lax.all_gather(ffn_params, "fsdp", axis=0, tiled=True), ffn_layout())
    grad_second, query_grads = ffn_backward(grad_query_final, query_kept, ffn_back[:6])
    grad_text, text_grads = ffn_backward(grad_text_final, text_kept, ffn_back[6:])
    ffn_flat_grad = join_flat(query_grads + text_grads, ffn_full.shape[0])
    ffn_grad = lax.psum_scatter(
        regroup(ffn_flat_grad), ("dp", "fsdp"), scatter_dimension=0, tiled=True
    )
    cross_back = split_flat(
        lax.all_gather(cross_params, "fsdp", axis=0, tiled=True), cross_layout()
    )
    grad_summed_two, grad_gain_two, grad_shift_two = norm_backward(
        summed_two, cross_back[7], cross_back[8], grad_second
    )
    grad_cross_out = grad_summed_two.astype(jnp.bfloat16)
    grad_cross_wo, grad_cross_bo, grad_cross_ctx = linear_back(
        cross_low, cross_back[3], grad_cross_out
    )
    grad_cq, grad_ck, grad_cv = attend_back(
        heads(cross_query, items),
        heads(cross_key, items),
        heads(cross_value, items),
        None,
        cross_top,
        heads(grad_cross_ctx.astype(jnp.bfloat16), items),
    )
    grad_cq = grad_cq.reshape(-1, width).astype(jnp.bfloat16)
    grad_ck = grad_ck.reshape(-1, width).astype(jnp.bfloat16)
    grad_cv = grad_cv.reshape(-1, width).astype(jnp.bfloat16)
    grad_cross_wq, grad_cross_bq, grad_query_in = linear_back(query_in, cross_back[0], grad_cq)
    grad_cross_wk = matmul_left(image_rows, grad_ck)
    grad_cross_wv = matmul_left(image_rows, grad_cv)
    grad_cross_bv = column_sum(grad_cv)
    grad_query_rows = grad_summed_two + grad_query_in
    cross_list = [
        grad_cross_wq,
        grad_cross_wk,
        grad_cross_wv,
        grad_cross_wo,
        grad_cross_bq,
        grad_cross_bv,
        grad_cross_bo,
        grad_gain_two,
        grad_shift_two,
    ]
    cross_flat_grad = join_flat(cross_list, cross_full.shape[0])
    cross_grad = lax.psum_scatter(
        regroup(cross_flat_grad), ("dp", "fsdp"), scatter_dimension=0, tiled=True
    )
    self_back = split_flat(lax.all_gather(self_params, "fsdp", axis=0, tiled=True), self_layout())
    grad_first = jnp.concatenate(
        [grad_query_rows.reshape(items, NQ, width), grad_text.reshape(items, -1, width)], 1
    ).reshape(-1, width)
    grad_summed_one, grad_gain_one, grad_shift_one = norm_backward(
        summed_one, self_back[7], self_back[8], grad_first
    )
    grad_attn = grad_summed_one.astype(jnp.bfloat16)
    grad_w_o, grad_b_o, grad_ctx = linear_back(context_low, self_back[3], grad_attn)
    grad_q, grad_k, grad_v = attend_back(
        heads(query_low, items),
        heads(key_low, items),
        heads(value_low, items),
        allowed,
        self_top,
        heads(grad_ctx.astype(jnp.bfloat16), items),
    )
    grad_q = grad_q.reshape(-1, width).astype(jnp.bfloat16)
    grad_k = grad_k.reshape(-1, width).astype(jnp.bfloat16)
    grad_v = grad_v.reshape(-1, width).astype(jnp.bfloat16)
    grad_w_q, grad_b_q, input_from_q = linear_back(inputs, self_back[0], grad_q)
    grad_w_k = matmul_left(inputs, grad_k)
    input_from_k = matmul_right(grad_k, self_back[1])
    grad_w_v, grad_b_v, input_from_v = linear_back(inputs, self_back[2], grad_v)
    hidden_grad = (
        (grad_summed_one + input_from_q + input_from_k + input_from_v)
        .reshape(items, seq, width)
        .astype(jnp.bfloat16)
    )
    self_list = [
        grad_w_q,
        grad_w_k,
        grad_w_v,
        grad_w_o,
        grad_b_q,
        grad_b_v,
        grad_b_o,
        grad_gain_one,
        grad_shift_one,
    ]
    self_flat_grad = join_flat(self_list, self_full.shape[0])
    self_grad = lax.psum_scatter(
        regroup(self_flat_grad), ("dp", "fsdp"), scatter_dimension=0, tiled=True
    )
    self_grad, cross_grad, ffn_grad = (
        lax.all_gather(self_grad.astype(jnp.bfloat16), "dp", axis=0, tiled=True).astype(
            self_grad.dtype
        ),
        lax.all_gather(cross_grad.astype(jnp.bfloat16), "dp", axis=0, tiled=True).astype(
            cross_grad.dtype
        ),
        lax.all_gather(ffn_grad.astype(jnp.bfloat16), "dp", axis=0, tiled=True).astype(
            ffn_grad.dtype
        ),
    )
    return (mixed, hidden_grad, self_grad, cross_grad, ffn_grad)


def solution(mesh):
    return jax.shard_map(
        per_device,
        mesh=mesh,
        in_specs=(
            P(("dp", "fsdp"), None, None),
            P(("dp", "fsdp")),
            P(("dp", "fsdp"), None, None),
            P(("dp", "fsdp"), None, None),
            P("fsdp"),
            P("fsdp"),
            P("fsdp"),
        ),
        out_specs=(
            P(("dp", "fsdp"), None, None),
            P(("dp", "fsdp"), None, None),
            P("fsdp"),
            P("fsdp"),
            P("fsdp"),
        ),
        check_vma=False,
    )
```

profile of v0, /device:TPU:0, one launch (start us, length us, event | category | flops | bytes accessed | tf_op | source)
XLA Modules:
  0.0 2604.6 jit_solution(10896527017699016095)
XLA Ops:
  17.5 14.2 reshape.500
  35.5 60.6 %all-gather.11.cloned.1.call-done = bf16[16,1,147712]{2,1,0:T(2,128)(2,1)} async-done(((bf16[1,1,147712]{2,1,0:T(2,128)(2,1)}), bf16[16,1,147712]{2,1,0:T(2,128)(2,1)}) %all-gather.11.cloned.1.call-update) | async-done | bytes 4726800 | tf_op jit(solution)/shard_map/all_gather | solution.py:156
  96.1 78.1 %reduce.11 = bf16[16,147712]{1,0:T(8,128)(2,1)} reduce(bf16[16,1,147712]{2,1,0:T(2,128)(2,1)} %all-gather.11.cloned.1.call-done, bf16[]{:T(256)} %constant.79), dimensions={1}, to_apply=%all-gather.reduce_sub_computation | reduce | bytes 9453570 | tf_op jit(solution)/shard_map/all_gather | solution.py:156
  174.2 10.1 reshape.497
  209.2 141.5 %reduce.12 = bf16[16,209152]{1,0:T(8,128)(2,1)} reduce(bf16[16,1,209152]{2,1,0:T(2,128)(2,1)} %all-gather.13.cloned.1.call-done, bf16[]{:T(256)} %constant.79), dimensions={1}, to_apply=%all-gather.1.reduce_sub_computation | reduce | bytes 13385730 | tf_op jit(solution)/shard_map/all_gather | solution.py:179
  350.8 14.0 reshape.499
  420.2 400.6 %reduce.13 = bf16[16,590592]{1,0:T(8,128)(2,1)} reduce(bf16[16,1,590592]{2,1,0:T(2,128)(2,1)} %all-gather.15.cloned.1.call-done, bf16[]{:T(256)} %constant.79), dimensions={1}, to_apply=%all-gather.2.reduce_sub_computation | reduce | bytes 37797888 | tf_op jit(solution)/shard_map/all_gather | solution.py:195
  820.8 43.1 %reshape.501 = bf16[9449472]{0:T(1024)(128)(2,1)} reshape(bf16[16,590592]{1,0:T(8,128)(2,1)} %reduce.13) | data formatting | bytes 37797888
  863.9 14.0 fusion.71
  880.7 8.2 slice.166
  888.9 9.2 slice.169
  913.7 9.3 slice.177
  1038.7 8.6 pad.12
  1047.3 10.3 reshape.482
  1138.5 10.0 pad.13
  1148.6 13.4 reshape.488
  1162.0 10.4 copy.156
  1172.4 9.8 reshape.489
  1192.0 10.8 reshape.491
  1210.0 10.8 reshape.493
  1221.4 8.3 constant_dynamic-update-slice_fusion.6
  1233.6 80.5 %dynamic-update-slice.6 = f32[9447936]{0:T(1024)} dynamic-update-slice(f32[9447936]{0:T(1024)} %constant_dynamic-update-slice_fusion.25, f32[2359296]{0:T(1024)} %bitcast.168, s32[]{} %constant.91) | dynamic-update-slice | bytes 18874372
  1315.4 80.5 %dynamic-update-slice.8 = f32[9447936]{0:T(1024)} dynamic-update-slice(f32[9447936]{0:T(1024)} %constant_dynamic-update-slice_fusion.24, f32[2359296]{0:T(1024)} %reshape.493, s32[]{} %constant.93) | dynamic-update-slice | bytes 18874372
  1399.8 27.1 %pad.14 = f32[9449472]{0:T(1024)} pad(f32[9447936]{0:T(1024)} %constant_dynamic-update-slice_fusion.21, f32[]{:T(128)} %constant.23.clone.1), padding=0_1536 | pad | bytes 75589632 | tf_op jit(solution)/shard_map/jit(_pad)/pad | solution.py:42
  1426.9 59.6 %reshape.494 = f32[16,2,295296]{2,1,0:T(2,128)} reshape(f32[9449472]{0:T(1024)} %pad.14) | data formatting | bytes 75595776 | tf_op jit(solution)/shard_map/reshape | solution.py:48
  1486.5 29.9 %copy.157 = f32[2,16,295296]{2,1,0:T(8,128)} copy(f32[2,16,295296]{2,0,1:T(2,128)} %bitcast.161) | data formatting | bytes 75595776 | tf_op jit(solution)/shard_map/transpose | solution.py:48
  1516.4 31.6 %reshape.495 = f32[9449472]{0:T(1024)} reshape(f32[2,16,295296]{2,1,0:T(8,128)} %copy.157) | data formatting | bytes 75595776 | tf_op jit(solution)/shard_map/reshape | solution.py:48
  1548.0 960.9 %all-reduce.8 = (bf16[2363392]{0:T(1024)(128)(2,1)}, bf16[3346432]{0:T(1024)(128)(2,1)}, bf16[9449472]{0:T(1024)(128)(2,1)}) all-reduce(f32[2363392]{0:T(1024)} %reshape.483, f32[3346432]{0:T(1024)} %reshape.489, f32[9449472]{0:T(1024)} %reshape.495), channel_id=2, replica_groups=mesh['dp'=2,'fsdp'=16] {'dp','fsdp'}, use_global_device_ids=true, to_apply=%region_28.29.clone | all-reduce | flops 15159296 | bytes 90955776
  2510.1 8.6 all-gather.3
  2531.3 14.9 all-gather.4
  2557.1 10.7 all-gather.17.cloned.1.call-done
  2567.8 26.9 %convert_reduce_fusion = f32[2,295296]{1,0:T(2,128)S(1)} fusion(bf16[2,1,295296]{2,1,0:T(2,128)(2,1)} %all-gather.17.cloned.1.call-done), kind=kLoop, calls=%fused_computation.6 | loop fusion | flops 590592 | bytes 3543552 | tf_op jit(solution)/shard_map/convert_element_type | solution.py:304
  (488 shorter events, 362.6 us)
Async XLA Ops:
  7.2 10.3 copy-start.56
  7.2 88.9 %all-gather.11.cloned.1.call-start = ((), (), s32[]{:S(2)}) async-start(), calls=%async_computation | async-start | bytes 10044416 | tf_op jit(solution)/shard_map/all_gather | solution.py:156
  11.7 197.5 %all-gather.13.cloned.1.call-start = ((), (), s32[]{:S(2)}) async-start(), calls=%async_computation.1 | async-start | bytes 14222336 | tf_op jit(solution)/shard_map/all_gather | solution.py:179
  17.4 14.4 copy-start.34
  17.4 402.8 %all-gather.15.cloned.1.call-start = ((), (), s32[]{:S(2)}) async-start(), calls=%async_computation.2 | async-start | bytes 40160256 | tf_op jit(solution)/shard_map/all_gather | solution.py:195
  31.7 2536.1 %all-gather.17.cloned.1.call-start = ((), (), s32[]{:S(2)}) async-start(), calls=%async_computation.3 | async-start | bytes 3543552 | tf_op jit(solution)/shard_map/all_gather | solution.py:304
  204.9 145.9 %copy-start.7 = (bf16[768,768]{1,0:T(8,128)(2,1)}, bf16[768,768]{1,0:T(8,128)(2,1)S(1)}, u32[]{:S(2)}) copy-start(bf16[768,768]{1,0:T(8,128)(2,1)S(1)} %reshape.456) | copy-start | bytes 3538948
  207.8 143.0 %copy-start.44 = (f32[2,32,768]{2,1,0:T(8,128)}, f32[2,32,768]{2,1,0:T(8,128)S(1)}, u32[]{:S(2)}) copy-start(f32[2,32,768]{2,1,0:T(8,128)S(1)} %get-tuple-element.72) | copy-start | bytes 589828
  208.6 196.8 %copy-start.59 = (bf16[2,32,768]{2,1,0:T(8,128)(2,1)}, bf16[2,32,768]{2,1,0:T(8,128)(2,1)S(1)}, u32[]{:S(2)}) copy-start(bf16[2,32,768]{2,1,0:T(8,128)(2,1)S(1)} %get-tuple-element.69) | copy-start | bytes 294916
  898.2 12.2 slice-start.2
  901.8 8.5 slice-start.3
  992.6 12.9 copy-start.40
  994.2 19.5 copy-start.46
  1031.3 6.8 copy-start.95
  1031.3 6.8 copy-start.96
  1131.2 6.8 copy-start.106
  1192.0 10.8 copy-start.51
  1192.0 10.8 copy-start.64
  1210.0 10.8 copy-start.113
  1221.4 8.3 copy-start.103
  1221.4 9.6 copy-start.102
  1221.4 11.0 copy-start.101
  1233.6 80.5 %copy-start.114 = (f32[3072]{0:T(1024)S(1)}, f32[3072]{0:T(1024)}, u32[]{:S(2)}) copy-start(f32[3072]{0:T(1024)} %get-tuple-element.21) | copy-start | bytes 36868
  1315.4 80.5 %copy-start.105 = (f32[768]{0:T(1024)S(1)}, f32[768]{0:T(1024)}, u32[]{:S(2)}) copy-start(f32[768]{0:T(1024)} %get-tuple-element.19) | copy-start | bytes 9220
  1315.4 81.8 %copy-start.104 = (f32[768]{0:T(1024)S(1)}, f32[768]{0:T(1024)}, u32[]{:S(2)}) copy-start(f32[768]{0:T(1024)} %get-tuple-element.7) | copy-start | bytes 9220
  1315.4 83.1 %copy-start.100 = (f32[768]{0:T(1024)S(1)}, f32[768]{0:T(1024)}, u32[]{:S(2)}) copy-start(f32[768]{0:T(1024)} %get-tuple-element.13) | copy-start | bytes 9220
  2546.2 8.5 copy-start.4
  2546.2 8.5 copy-start.30
  2546.2 8.5 copy-start.39
  2546.2 8.5 copy-start.122
  2547.5 6.5 copy-start.75
  2547.5 6.5 copy-start.76
  (107 other events, 326.7 us)
Sparse Core Ops, SparseCore 0:
  11.8 84.2 all-gather.10
  98.9 103.9 all-gather.12
  205.1 186.1 all-gather.14
  2531.4 36.2 all-gather.16
where the time goes:
time: 2630 us; the launch traced here: 2600 us
  blocking collectives  984 us (37%)
  local copies, waits for them, and re-layouts  767 us (29%)
  other arithmetic  672 us (26%)
  matrix products  94.1 us (4%)
  waiting for transfers between devices  71.3 us (3%)
    unnamed x1, blocking collectives  961 us
    all_gather x1, other arithmetic, per_device(): ffn_full = lax.all_gather(ffn_params, 'fsdp', axis=0, tiled=True)  401 us
    unnamed x312, local copies, waits for them, and re-layouts  337 us
    all_gather x1, other arithmetic, per_device(): cross_full = lax.all_gather(cross_params, 'fsdp', axis=0, tiled=True)  142 us
    reshape x6, local copies, waits for them, and re-layouts, regroup(): return flat_vec.reshape(groups, replicas, -1).transpose(1, 0, 2).reshape(-1)  133 us
    all_gather x1, other arithmetic, per_device(): self_full = lax.all_gather(self_params, 'fsdp', axis=0, tiled=True)  78.1 us
    all_gather x1, waiting for transfers between devices, per_device(): self_full = lax.all_gather(self_params, 'fsdp', axis=0, tiled=True)  60.6 us
  transfers between devices with their start and end apart: 4, of which 2 were waited for; matrix products, arithmetic and copies ran while one was open for 14% of the time, Pallas kernels for 0%

commit v1 on v0

--- a/solution.py
+++ b/solution.py
@@ -176,7 +176,19 @@
     first_items = first.reshape(items, seq, width)
     query_rows = first_items[:, :NQ].reshape(-1, width)
     text_rows = first_items[:, NQ:].reshape(-1, width)
-    cross_full = lax.all_gather(cross_params, "fsdp", axis=0, tiled=True)
+    near = lax.axis_size("fsdp")
+    v_now = lax.axis_index("fsdp")
+    long_array, tmp = (near, v_now)
+    cross_full, out_arr = (cross_params, 1)
+    while out_arr < long_array:
+        kept_rows = []
+        for k in range(long_array):
+            kept_rows.append((k, k ^ out_arr))
+        wide_out = lax.ppermute(cross_full, "fsdp", perm=kept_rows)
+        o_now = jnp.concatenate([cross_full, wide_out], axis=0)
+        t1 = jnp.concatenate([wide_out, cross_full], axis=0)
+        cross_full = jnp.where(tmp & out_arr == 0, o_now, t1)
+        out_arr = 2 * out_arr
     cross_parts = split_flat(cross_full, cross_layout())
     cross_wq, cross_wk, cross_wv, cross_wo, cross_bq, cross_bv, cross_bo, gain_two, shift_two = (
         cross_parts

time: 2630 us -> 2940 us (1.12)
  waiting for transfers between devices: 71.3 us -> 317 us
  other arithmetic: 672 us -> 713 us
    ppermute x0 -> x4, waiting for transfers between devices: none -> 311 us  [per_device(): wide_out = lax.ppermute(cross_full, 'fsdp', perm=kept_rows)]
    all_gather x1, waiting for transfers between devices: 60.6 us -> 0.01 us  [per_device(): self_full = lax.all_gather(self_params, 'fsdp', axis=0, tiled=True)]
    select_n x0 -> x4, other arithmetic: none -> 33.8 us  [per_device(): cross_full = jnp.where(tmp & out_arr == 0, o_now, t1)]
    unnamed x312 -> x290, local copies, waits for them, and re-layouts: 337 us -> 340 us
  transfers between devices with their start and end apart: 4 -> 8, of which waited for: 2 -> 5; matrix products, arithmetic and copies ran while one was open for 14% -> 14% of each run, Pallas kernels for 0% -> 0%
where the time goes in v1:
time: 2940 us; the launch traced here: 2920 us
  blocking collectives  980 us (33%)
  local copies, waits for them, and re-layouts  790 us (27%)
  other arithmetic  713 us (24%)
  waiting for transfers between devices  317 us (11%)
  matrix products  96.1 us (3%)
    unnamed x1, blocking collectives  955 us
    all_gather x1, other arithmetic, per_device(): ffn_full = lax.all_gather(ffn_params, 'fsdp', axis=0, tiled=True)  401 us
    unnamed x290, local copies, waits for them, and re-layouts  340 us
    ppermute x4, waiting for transfers between devices, per_device(): wide_out = lax.ppermute(cross_full, 'fsdp', perm=kept_rows)  311 us
    all_gather x1, other arithmetic, per_device(): lax.all_gather(cross_params, 'fsdp', axis=0, tiled=True)  142 us
    reshape x6, local copies, waits for them, and re-layouts, regroup(): return flat_vec.reshape(groups, replicas, -1).transpose(1, 0, 2).reshape(-1)  132 us
    all_gather x1, other arithmetic, per_device(): self_full = lax.all_gather(self_params, 'fsdp', axis=0, tiled=True)  77.5 us
  transfers between devices with their start and end apart: 8, of which 5 were waited for; matrix products, arithmetic and copies ran while one was open for 14% of the time, Pallas kernels for 0%

profile of v1, /device:TPU:0, one launch (start us, length us, event | category | flops | bytes accessed | tf_op | source)
XLA Modules:
  0.0 2918.3 jit_solution(11994993512006377959)
XLA Ops:
  18.3 19.1 collective-permute-done.1
  46.7 77.1 %collective-permute-done.2 = bf16[836608]{0:T(1024)(128)(2,1)} collective-permute-done((bf16[836608]{0:T(1024)(128)(2,1)S(1)}, bf16[836608]{0:T(1024)(128)(2,1)}, u32[]{:S(2)}, u32[]{:S(2)}) %collective-permute-start.2) | collective-permute-done | bytes 1673248 | tf_op jit(solution)/shard_map/ppermute | solution.py:187
  130.0 14.2 reshape.505
  154.2 212.8 %collective-permute-done.3 = bf16[1673216]{0:T(1024)(128)(2,1)} collective-permute-done((bf16[1673216]{0:T(1024)(128)(2,1)S(1)}, bf16[1673216]{0:T(1024)(128)(2,1)}, u32[]{:S(2)}, u32[]{:S(2)}) %collective-permute-start.3) | collective-permute-done | bytes 3346464 | tf_op jit(solution)/shard_map/ppermute | solution.py:187
  367.0 24.8 maximum_select_fusion
  429.9 77.5 %reduce.11 = bf16[16,147712]{1,0:T(8,128)(2,1)} reduce(bf16[16,1,147712]{2,1,0:T(2,128)(2,1)} %all-gather.11.cloned.1.call-done, bf16[]{:T(256)} %constant.92), dimensions={1}, to_apply=%all-gather.reduce_sub_computation | reduce | bytes 9453570 | tf_op jit(solution)/shard_map/all_gather | solution.py:156
  507.4 10.4 reshape.504
  564.1 141.5 %reduce.13 = bf16[16,209152]{1,0:T(8,128)(2,1)} reduce(bf16[16,1,209152]{2,1,0:T(2,128)(2,1)} %all-gather.15.cloned.1.call-done, bf16[]{:T(256)} %constant.92), dimensions={1}, to_apply=%all-gather.2.reduce_sub_computation | reduce | bytes 13385730 | tf_op jit(solution)/shard_map/all_gather | solution.py:225
  705.6 13.7 reshape.508
  730.5 400.9 %reduce.12 = bf16[16,590592]{1,0:T(8,128)(2,1)} reduce(bf16[16,1,590592]{2,1,0:T(2,128)(2,1)} %all-gather.13.cloned.1.call-done, bf16[]{:T(256)} %constant.92), dimensions={1}, to_apply=%all-gather.1.reduce_sub_computation | reduce | bytes 37797888 | tf_op jit(solution)/shard_map/all_gather | solution.py:207
  1131.3 43.2 %reshape.506 = bf16[9449472]{0:T(1024)(128)(2,1)} reshape(bf16[16,590592]{1,0:T(8,128)(2,1)} %reduce.12) | data formatting | bytes 37797888
  1174.5 14.1 fusion.73
  1199.5 9.3 slice.175
  1222.0 9.3 slice.183
  1354.2 8.7 pad.12
  1362.9 10.3 reshape.489
  1457.0 10.1 pad.13
  1467.0 13.3 reshape.495
  1480.4 10.4 copy.156
  1490.8 10.0 reshape.496
  1510.4 10.8 reshape.498
  1528.3 10.8 reshape.500
  1551.9 80.4 %dynamic-update-slice.6 = f32[9447936]{0:T(1024)} dynamic-update-slice(f32[9447936]{0:T(1024)} %constant_dynamic-update-slice_fusion.25, f32[2359296]{0:T(1024)} %bitcast.172, s32[]{} %constant.104) | dynamic-update-slice | bytes 18874372
  1633.6 80.4 %dynamic-update-slice.8 = f32[9447936]{0:T(1024)} dynamic-update-slice(f32[9447936]{0:T(1024)} %constant_dynamic-update-slice_fusion.24, f32[2359296]{0:T(1024)} %reshape.500, s32[]{} %constant.106) | dynamic-update-slice | bytes 18874372
  1717.9 27.0 pad.14
  1744.9 59.4 %reshape.501 = f32[16,2,295296]{2,1,0:T(2,128)} reshape(f32[9449472]{0:T(1024)} %pad.14) | data formatting | bytes 75595776 | tf_op jit(solution)/shard_map/reshape | solution.py:48
  1804.4 29.9 %copy.157 = f32[2,16,295296]{2,1,0:T(8,128)} copy(f32[2,16,295296]{2,0,1:T(2,128)} %bitcast.165) | data formatting | bytes 75595776 | tf_op jit(solution)/shard_map/transpose | solution.py:48
  1834.3 31.6 %reshape.502 = f32[9449472]{0:T(1024)} reshape(f32[2,16,295296]{2,1,0:T(8,128)} %copy.157) | data formatting | bytes 75595776 | tf_op jit(solution)/shard_map/reshape | solution.py:48
  1865.9 955.3 %all-reduce.8 = (bf16[2363392]{0:T(1024)(128)(2,1)}, bf16[3346432]{0:T(1024)(128)(2,1)}, bf16[9449472]{0:T(1024)(128)(2,1)}) all-reduce(f32[2363392]{0:T(1024)} %reshape.490, f32[3346432]{0:T(1024)} %reshape.496, f32[9449472]{0:T(1024)} %reshape.502), channel_id=2, replica_groups=mesh['dp'=2,'fsdp'=16] {'dp','fsdp'}, use_global_device_ids=true, to_apply=%region_28.29.clone | all-reduce | flops 15159296 | bytes 90955776
  2822.4 8.6 all-gather.3
  2844.2 15.8 all-gather.4
  2881.1 26.9 convert_reduce_fusion
  (482 shorter events, 435.5 us)
Async XLA Ops:
  7.2 34.0 %copy-start.43 = (bf16[209152]{0:T(1024)(128)(2,1)S(1)}, bf16[209152]{0:T(1024)(128)(2,1)}, u32[]{:S(2)}) copy-start(bf16[209152]{0:T(1024)(128)(2,1)} %param.12) | copy-start | bytes 1254916
  7.2 422.7 %all-gather.11.cloned.1.call-start = ((), (), s32[]{:S(2)}) async-start(), calls=%async_computation | async-start | bytes 10044416 | tf_op jit(solution)/shard_map/all_gather | solution.py:156
  7.2 2.1 collective-permute-start
  10.9 26.5 collective-permute-start.1
  18.2 545.8 %all-gather.15.cloned.1.call-start = ((), (), s32[]{:S(2)}) async-start(), calls=%async_computation.2 | async-start | bytes 14222336 | tf_op jit(solution)/shard_map/all_gather | solution.py:225
  39.5 84.3 %collective-permute-start.2 = (bf16[836608]{0:T(1024)(128)(2,1)S(1)}, bf16[836608]{0:T(1024)(128)(2,1)}, u32[]{:S(2)}, u32[]{:S(2)}) collective-permute-start(bf16[836608]{0:T(1024)(128)(2,1)S(1)} %maximum_select_fusion.2), channel_id=1, source_target_pairs={{0,4},{1,5},{2,6},{3,7},{4,0},{5,1},{6,2},{7,3},{8,12},{9,13},{10,... | collective-permute-start | bytes 5019656 | tf_op jit(solution)/shard_map/ppermute | solution.py:187
  46.6 683.8 %all-gather.13.cloned.1.call-start = ((), (), s32[]{:S(2)}) async-start(), calls=%async_computation.1 | async-start | bytes 40160256 | tf_op jit(solution)/shard_map/all_gather | solution.py:207
  46.7 83.3 %copy-start.52 = (bf16[590592]{0:T(1024)(128)(2,1)S(1)}, bf16[590592]{0:T(1024)(128)(2,1)}, u32[]{:S(2)}) copy-start(bf16[590592]{0:T(1024)(128)(2,1)} %param.13) | copy-start | bytes 3543556
  129.2 237.8 %collective-permute-start.3 = (bf16[1673216]{0:T(1024)(128)(2,1)S(1)}, bf16[1673216]{0:T(1024)(128)(2,1)}, u32[]{:S(2)}, u32[]{:S(2)}) collective-permute-start(bf16[1673216]{0:T(1024)(128)(2,1)S(1)} %maximum_select_fusion.1), channel_id=1, source_target_pairs={{0,8},{1,9},{2,10},{3,11},{4,12},{5,13},{6,14},{7,15},{8,0},{9,1},... | collective-permute-start | bytes 10039304 | tf_op jit(solution)/shard_map/ppermute | solution.py:187
  144.2 2736.9 %all-gather.17.cloned.1.call-start = ((), (), s32[]{:S(2)}) async-start(), calls=%async_computation.3 | async-start | bytes 3543552 | tf_op jit(solution)/shard_map/all_gather | solution.py:316
  144.7 7.9 copy-start.117
  404.5 8.3 copy-start.51
  517.7 8.6 copy-start.12
  542.0 9.0 copy-start.33
  1208.8 9.8 slice-start.2
  1260.2 11.5 copy-start.7
  1305.0 9.7 copy-start.35
  1306.6 14.6 copy-start.36
  1309.8 19.5 copy-start.41
  1510.4 10.8 copy-start.47
  1510.4 10.8 copy-start.60
  1528.3 10.8 copy-start.105
  1539.7 8.3 copy-start.94
  1539.7 9.6 copy-start.93
  1539.7 10.9 copy-start.92
  1551.9 80.4 %copy-start.106 = (f32[3072]{0:T(1024)S(1)}, f32[3072]{0:T(1024)}, u32[]{:S(2)}) copy-start(f32[3072]{0:T(1024)} %get-tuple-element.21) | copy-start | bytes 36868
  1633.6 80.4 %copy-start.97 = (f32[768]{0:T(1024)S(1)}, f32[768]{0:T(1024)}, u32[]{:S(2)}) copy-start(f32[768]{0:T(1024)} %get-tuple-element.19) | copy-start | bytes 9220
  1633.6 81.7 %copy-start.95 = (f32[768]{0:T(1024)S(1)}, f32[768]{0:T(1024)}, u32[]{:S(2)}) copy-start(f32[768]{0:T(1024)} %get-tuple-element.7) | copy-start | bytes 9220
  1633.6 83.0 %copy-start.91 = (f32[768]{0:T(1024)S(1)}, f32[768]{0:T(1024)}, u32[]{:S(2)}) copy-start(f32[768]{0:T(1024)} %get-tuple-element.13) | copy-start | bytes 9220
  2844.2 26.4 copy-start.4
  2844.2 26.4 copy-start.112
  2860.0 12.3 copy-start.5
  (100 other events, 373.7 us)
Sparse Core Ops, SparseCore 0:
  18.4 106.8 all-gather.10
  128.1 207.9 all-gather.14
  338.2 197.5 all-gather.12
  2844.3 36.7 all-gather.16
